TPU v7x, 32 devices: a whole 2x2x4 slice. The times are simulated.
32 devices in a mesh: site: 4 (over y, core), blk: 8 (over z, x).
Axes of the slice: x: 2, y: 2, z: 4, core: 2. Of those that a mesh axis runs over, the one named last changes fastest.
Arguments:
- corner: bfloat16 [4, 48, 128, 128], P('site', 'blk')
- bcorner: bfloat16 [2, 4, 48, 128, 128], P(None, 'site', 'blk'), may hold values from -6 to 6
- edge: bfloat16 [4, 48, 128, 2304], P('site', 'blk'), may hold values from -0.5 to 0.5
- bedge: bfloat16 [4, 48, 128, 2304], P('site', 'blk'), may hold values from -0.5 to 0.5
- proj: bfloat16 [4, 48, 2304, 128], P('site', 'blk'), may hold values from -0.125 to 0.125
- joining: int32 [4, 48], P('site'), may hold values from 0 to 47, as said below
- momentum: float32 [1], replicated, may hold values from 0.5 to 2.5
Outputs:
- new_corner: bfloat16 [4, 48, 128, 128], P('site', 'blk')
- new_bcorner: bfloat16 [2, 4, 48, 128, 128], P(None, 'site', 'blk')
- momentum_sum: float32 [2, 48, 128, 128], P(None, 'blk', 'site')
Inputs may be any that keep to these rules, and one draw needn't show every extreme that they name: Each row of joining is a permutation of the 48 slots. The 6 new slots of one blk device take their blocks from the slots of at most 3 blk devices, exactly 2 from each of them.
All inputs are finite; a program needn't handle non-finite values. Where the computation divides by a largest or mean magnitude, that divisor is 1e-20 or more.
Results may differ from a plain program's by a relative error of at most 0.024.
Values may be sent and summed in bfloat16 or wider, within the bound.
No kernel may reach another device: no remote copies, remote signals or barrier semaphores. Data moves between devices by JAX's collectives and lax.ppermute only.
A program may use at most 128 MiB of HBM per device.

v0:
```python
import jax
import jax.numpy as jnp
from jax import lax
from jax.sharding import PartitionSpec as P

epsilon = 1e-06


def shifted(block, axis, distance):
    devices = range(lax.axis_size(axis))
    route = [((i - distance) % len(devices), i) for i in devices]
    return lax.ppermute(block, axis, route)


def product(left, right):
    return jnp.einsum("jmn,jnk->jmk", left, right, preferred_element_type=jnp.float32)


def per_device(corner, bcorner, edge, bedge, proj, joining, momentum):
    per_dev = corner.shape[1]
    my_blk = lax.axis_index("blk")
    my_site = lax.axis_index("site")
    left_corner, left_bcorner = shifted((corner, bcorner), "site", 1)
    corner_here = left_corner[0]
    column = edge[0]
    bcolumn = bedge[0]
    project = proj[0]
    enlarged = product(corner_here, column).astype(jnp.bfloat16)
    real_term = product(left_bcorner[0, 0], column)
    imag_term = product(left_bcorner[1, 0], column)
    inserted = product(corner_here, bcolumn)
    angle = momentum[0] * my_site.astype(jnp.float32)
    cosine = jnp.cos(angle)
    sine = jnp.sin(angle)
    excited_re = (cosine * real_term - sine * imag_term + inserted).astype(jnp.bfloat16)
    excited_im = (sine * real_term + cosine * imag_term).astype(jnp.bfloat16)
    projected = jnp.stack(
        [
            product(enlarged, project).astype(jnp.bfloat16),
            product(excited_re, project).astype(jnp.bfloat16),
            product(excited_im, project).astype(jnp.bfloat16),
        ],
        axis=1,
    )
    local_peak = jnp.max(jnp.abs(projected[:, 0].astype(jnp.float32)))
    peak = lax.pmax(local_peak, "blk")
    sources = lax.dynamic_slice_in_dim(joining[0], my_blk * per_dev, per_dev)
    piece = lax.all_gather(projected, "blk", axis=0, tiled=True)
    picks = (sources[:, None] == jnp.arange(piece.shape[0], dtype=jnp.int32)[None, :]).astype(
        jnp.bfloat16
    )
    routed = jnp.einsum("it,txmn->ixmn", picks, piece, preferred_element_type=jnp.float32)
    scaled = routed / (peak + epsilon)
    new_corner = scaled[:, 0].astype(jnp.bfloat16)
    new_b = jnp.stack([scaled[:, 1], scaled[:, 2]], axis=0).astype(jnp.bfloat16)
    summed = lax.psum_scatter(
        new_b.astype(jnp.float32).astype(jnp.bfloat16), "site", scatter_dimension=2, tiled=True
    ).astype(jnp.float32)
    return (new_corner[None], new_b[:, None], summed)


def solution(mesh):
    in_specs = (
        P("site", "blk", None, None),
        P(None, "site", "blk", None, None),
        P("site", "blk", None, None),
        P("site", "blk", None, None),
        P("site", "blk", None, None),
        P("site", None),
        P(),
    )
    out_specs = (
        P("site", "blk", None, None),
        P(None, "site", "blk", None, None),
        P(None, "blk", "site", None),
    )
    return jax.shard_map(
        per_device, mesh=mesh, in_specs=in_specs, out_specs=out_specs, check_vma=False
    )
```

profile of v0, /device:TPU:0, one launch (start us, length us, event | category | flops | bytes accessed | tf_op | source)
XLA Modules:
  0.0 171.9 jit_solution(4399224337403264530)
XLA Ops:
  7.2 0.0 copy-start
  7.2 0.0 all-gather.2.cloned.1.call-start
  7.2 0.5 collective-permute-start
  7.7 2.6 %collective-permute-start.1 = (bf16[2,1,6,128,128]{4,3,2,1,0:T(8,128)(2,1)}, bf16[2,1,6,128,128]{4,3,2,1,0:T(8,128)(2,1)}, u32[]{:S(2)}, u32[]{:S(2)}) collective-permute-start(bf16[2,1,6,128,128]{4,3,2,1,0:T(8,128)(2,1)} %param.8), channel_id=1, source_target_pairs={{24,0},{0,8},{8,16},{16,24},{25,1},{1,9},{9,17},{17,25},{26,2},{2,... | collective-permute-start | bytes 1179656 | tf_op jit(solution)/shard_map/ppermute | solution.py:12
  11.2 2.2 %collective-permute-done = bf16[1,6,128,128]{3,2,1,0:T(8,128)(2,1)} collective-permute-done((bf16[1,6,128,128]{3,2,1,0:T(8,128)(2,1)}, bf16[1,6,128,128]{3,2,1,0:T(8,128)(2,1)}, u32[]{:S(2)}, u32[]{:S(2)}) %collective-permute-start) | collective-permute-done | bytes 196640 | tf_op jit(solution)/shard_map/ppermute | solution.py:12
  13.4 0.0 copy-done
  13.4 5.5 %abs_reduce_fusion = (f32[]{:T(128)}, bf16[6,128,128]{2,1,0:T(8,128)(2,1)}) fusion(bf16[1,6,2304,128]{3,2,1,0:T(8,128)(2,1)} %param.11, bf16[1,6,128,2304]{3,2,1,0:T(8,128)(2,1)S(1)} %copy-done, bf16[1,6,128,128]{3,2,1,0:T(8,128)(2,1)} %collective-permute-done), kind=kOutput, calls=%fused_computation.34 | convolution fusion | flops 908132352 | bytes 7471108 | tf_op jit(solution)/shard_map/jmn,jnk->jmk/dot_general | solution.py:16
  18.8 0.0 collective-permute-done.1
  18.8 2.0 %fusion.10 = f32[6,128,2304]{2,1,0:T(8,128)S(1)} fusion(bf16[1,6,128,2304]{3,2,1,0:T(8,128)(2,1)S(1)} %copy-done, bf16[2,1,6,128,128]{4,3,2,1,0:T(8,128)(2,1)} %collective-permute-done.1), kind=kOutput, calls=%fused_computation.13 | convolution fusion | flops 452984832 | bytes 10813440 | tf_op jit(solution)/shard_map/jmn,jnk->jmk/dot_general | solution.py:16
  20.8 0.0 copy-start.1
  20.8 2.2 %fusion.12 = f32[6,128,2304]{2,1,0:T(8,128)S(1)} fusion(bf16[1,6,128,2304]{3,2,1,0:T(8,128)(2,1)S(1)} %copy-done, bf16[2,1,6,128,128]{4,3,2,1,0:T(8,128)(2,1)} %collective-permute-done.1), kind=kOutput, calls=%fused_computation.15 | convolution fusion | flops 452984832 | bytes 10813440 | tf_op jit(solution)/shard_map/jmn,jnk->jmk/dot_general | solution.py:16
  23.0 0.7 copy-done.1
  23.7 0.0 copy-start.2
  23.7 2.9 %copy-done.2 = f32[6,128,2304]{2,1,0:T(8,128)} copy-done((f32[6,128,2304]{2,1,0:T(8,128)}, f32[6,128,2304]{2,1,0:T(8,128)S(1)}, u32[]{:S(2)}) %copy-start.2) | copy-done | bytes 7077912
  26.7 4.0 %fusion.43 = bf16[6,1,128,128]{3,2,0,1:T(8,128)(2,1)} fusion(bf16[1,6,2304,128]{3,2,1,0:T(8,128)(2,1)} %param.11, f32[6,128,2304]{2,1,0:T(8,128)S(1)} %fusion.10, f32[6,128,2304]{2,1,0:T(8,128)S(1)} %fusion.12, f32[]{:T(128)S(6)} %sin.3, f32[]{:T(128)S(6)} %cos.3), kind=kOutput, calls=%fused_computation.26 | convolution fusion | flops 460161024 | bytes 17891336 | tf_op jit(solution)/shard_map/jmn,jnk->jmk/dot_general | solution.py:16
  30.7 0.0 copy-start.3
  30.7 10.1 %fusion.38 = bf16[6,1,128,128]{3,2,0,1:T(8,128)(2,1)} fusion(bf16[1,6,2304,128]{3,2,1,0:T(8,128)(2,1)} %param.11, f32[6,128,2304]{2,1,0:T(8,128)} %copy-done.1, f32[6,128,2304]{2,1,0:T(8,128)} %copy-done.2, f32[]{:T(128)S(6)} %sin.3, f32[]{:T(128)S(6)} %cos.3, bf16[1,6,128,2304]{3,2,1,0:T(8,128)(2,1)} %param.10, ...), kind=kOutput, calls=%fused_computation.25 | convolution fusion | flops 914915328 | bytes 21626888 | tf_op jit(solution)/shard_map/jmn,jnk->jmk/dot_general | solution.py:16
  40.8 2.0 %pad_maximum_fusion = bf16[6,3,128,128]{3,2,0,1:T(8,128)(2,1)} fusion(bf16[6,1,128,128]{3,2,0,1:T(8,128)(2,1)} %fusion.43, bf16[6,1,128,128]{3,2,0,1:T(8,128)(2,1)} %fusion.38, bf16[6,1,128,128]{3,2,0,1:T(8,128)(2,1)} %bitcast.83), kind=kLoop, calls=%fused_computation.28 | loop fusion | flops 589824 | bytes 1179648 | tf_op jit(solution)/shard_map/stack | solution.py:37
  42.8 0.0 all-gather.2.cloned.1.call-update
  42.8 0.0 all-reduce.3.cloned.1.call-start
  42.9 0.0 copy-done.3
  42.9 0.1 dynamic-slice_bitcast_fusion
  43.0 23.6 %pmax.7 = f32[]{:T(128)} all-reduce(f32[]{:T(128)} %get-tuple-element.14), channel_id=1, replica_groups=mesh['site'=4,'blk'=8] {'blk'}, use_global_device_ids=true, to_apply=%region_1.0 | all-reduce | flops 1 | bytes 8 | tf_op jit(solution)/shard_map/pmax | solution.py:46
  67.2 57.8 %all-gather.2.cloned.1.call-done = bf16[48,3,128,128]{3,2,0,1:T(8,128)(2,1)} async-done(((bf16[6,3,128,128]{3,2,0,1:T(8,128)(2,1)}), bf16[48,3,128,128]{3,2,0,1:T(8,128)(2,1)}) %all-gather.2.cloned.1.call-update) | async-done | bytes 4718608 | tf_op jit(solution)/shard_map/all_gather | solution.py:48
  125.0 5.0 %fusion.46 = bf16[6,3,128,128]{3,0,2,1:T(8,128)(2,1)S(1)} fusion(bf16[48,3,128,128]{3,2,0,1:T(8,128)(2,1)} %all-gather.2.cloned.1.call-done, f32[]{:T(128)S(6)} %add.17, s32[6]{0:T(128)S(1)} %dynamic-slice_bitcast_fusion), kind=kOutput, calls=%fused_computation.27 | convolution fusion | flops 28901664 | bytes 5308444 | tf_op jit(solution)/shard_map/it,txmn->ixmn/dot_general | solution.py:52
  130.1 0.0 copy-start.4
  130.1 1.0 fusion.54
  131.0 0.1 pad_maximum_fusion.2
  131.2 1.4 copy.15
  132.5 0.0 all-reduce.3.cloned.1.call-update
  132.6 0.0 copy-done.4
  132.6 0.6 dynamic-slice.1
  133.8 1.2 pad_maximum_fusion.1
  135.0 0.8 copy.17
  135.8 1.7 copy.16
  137.4 26.0 %all-reduce.3.cloned.1.call-done = bf16[2,6,128,128]{3,0,1,2:T(2,128)(2,1)} async-done(((bf16[2,6,128,128]{3,0,1,2:T(2,128)(2,1)}), bf16[2,6,128,128]{3,0,1,2:T(2,128)(2,1)}) %all-reduce.3.cloned.1.call-update) | async-done | bytes 393232
  163.4 1.0 dynamic-slice_convert_fusion
  164.4 0.7 copy.18
Async XLA Ops:
  7.2 6.2 %copy-start = (bf16[1,6,128,2304]{3,2,1,0:T(8,128)(2,1)S(1)}, bf16[1,6,128,2304]{3,2,1,0:T(8,128)(2,1)}, u32[]{:S(2)}) copy-start(bf16[1,6,128,2304]{3,2,1,0:T(8,128)(2,1)} %param.9) | copy-start | bytes 10616836
  7.2 117.9 %all-gather.2.cloned.1.call-start = ((), (), s32[]{:S(2)}) async-start(), calls=%async_computation | async-start | bytes 5308416 | tf_op jit(solution)/shard_map/all_gather | solution.py:48
  7.2 6.1 %collective-permute-start = (bf16[1,6,128,128]{3,2,1,0:T(8,128)(2,1)}, bf16[1,6,128,128]{3,2,1,0:T(8,128)(2,1)}, u32[]{:S(2)}, u32[]{:S(2)}) collective-permute-start(bf16[1,6,128,128]{3,2,1,0:T(8,128)(2,1)} %param.7), channel_id=1, source_target_pairs={{24,0},{0,8},{8,16},{16,24},{25,1},{1,9},{9,17},{17,25},{26,2},{2,... | collective-permute-start | bytes 589832 | tf_op jit(solution)/shard_map/ppermute | solution.py:12
  7.7 11.1 %collective-permute-start.1 = (bf16[2,1,6,128,128]{4,3,2,1,0:T(8,128)(2,1)}, bf16[2,1,6,128,128]{4,3,2,1,0:T(8,128)(2,1)}, u32[]{:S(2)}, u32[]{:S(2)}) collective-permute-start(bf16[2,1,6,128,128]{4,3,2,1,0:T(8,128)(2,1)} %param.8), channel_id=1, source_target_pairs={{24,0},{0,8},{8,16},{16,24},{25,1},{1,9},{9,17},{17,25},{26,2},{2,... | collective-permute-start | bytes 1179656 | tf_op jit(solution)/shard_map/ppermute | solution.py:12
  20.8 2.9 %copy-start.1 = (f32[6,128,2304]{2,1,0:T(8,128)}, f32[6,128,2304]{2,1,0:T(8,128)S(1)}, u32[]{:S(2)}) copy-start(f32[6,128,2304]{2,1,0:T(8,128)S(1)} %fusion.10) | copy-start | bytes 21233668
  23.7 2.9 %copy-start.2 = (f32[6,128,2304]{2,1,0:T(8,128)}, f32[6,128,2304]{2,1,0:T(8,128)S(1)}, u32[]{:S(2)}) copy-start(f32[6,128,2304]{2,1,0:T(8,128)S(1)} %fusion.12) | copy-start | bytes 21233668
  30.7 12.2 %copy-start.3 = (s32[1,48]{1,0:T(1,128)S(1)}, s32[1,48]{1,0:T(1,128)}, u32[]{:S(2)}) copy-start(s32[1,48]{1,0:T(1,128)} %param.12) | copy-start | bytes 580
  42.8 120.6 %all-reduce.3.cloned.1.call-start = ((), (), s32[]{:S(2)}) async-start(), calls=%async_computation.1 | async-start | bytes 786432
  130.1 2.5 %copy-start.4 = (u32[32]{0:T(128)S(1)}, u32[32]{0:T(128)}, u32[]{:S(2)}) copy-start(u32[32]{0:T(128)} %constant.27) | copy-start | bytes 388
Sparse Core Ops, SparseCore 0:
  42.9 82.0 all-gather.1
  132.7 30.7 all-reduce.2
where the time goes:
time: 172 us
  waiting for transfers between devices  86.1 us (50%)
  matrix products  28.8 us (17%)
  blocking collectives  23.6 us (14%)
  between operations  16.2 us (9%)
  local copies, waits for them, and re-layouts  9.82 us (6%)
  other arithmetic  4.23 us (2%)
  starting transfers between devices  3.21 us (2%)
    all_gather x1, waiting for transfers between devices, per_device(): piece = lax.all_gather(projected, 'blk', axis=0, tiled=True)  57.8 us
    unnamed x3, waiting for transfers between devices  26.1 us
    dot_general x5, matrix products, product(): jnp.einsum('jmn,jnk->jmk', left, right, preferred_element_type=jnp.float32)  23.8 us
    pmax x1, blocking collectives, per_device(): peak = lax.pmax(local_peak, 'blk')  23.6 us
    unnamed x14, local copies, waits for them, and re-layouts  7.4 us
    dot_general x1, matrix products, per_device(): jnp.einsum('it,txmn->ixmn', picks, piece, preferred_element_type=jnp.floa...  5.01 us
  transfers between devices with their start and end apart: 4, of which 3 were waited for; matrix products, arithmetic and copies ran while one was open for 6% of the time, Pallas kernels for 0%

commit v1 on v0

v1 whole, which is shorter than its diff:
```python
import jax
import jax.numpy as jnp
from jax import lax
from jax.experimental import pallas as pl
from jax.experimental.pallas import tpu as pltpu
from jax.sharding import PartitionSpec as P

epsilon = 1e-06


def shifted(block, axis, distance):
    devices = range(lax.axis_size(axis))
    route = [((i - distance) % len(devices), i) for i in devices]
    return lax.ppermute(block, axis, route)


def edge_proj_kernel(edge_ref, bedge_ref, proj_ref, w_ref, v_ref):
    project = proj_ref[0, 0]
    w_ref[0] = jnp.dot(edge_ref[0, 0], project, preferred_element_type=jnp.float32).astype(w_ref.dtype)
    v_ref[0] = jnp.dot(bedge_ref[0, 0], project, preferred_element_type=jnp.float32).astype(v_ref.dtype)


def edge_proj(edge, bedge, proj):
    _, slots, m, k = edge.shape
    block = jax.ShapeDtypeStruct((slots, m, m), jnp.bfloat16)
    return pl.pallas_call(
        edge_proj_kernel,
        grid=(slots,),
        out_shape=(block, block),
        in_specs=[
            pl.BlockSpec((1, 1, m, k), lambda i: (0, i, 0, 0)),
            pl.BlockSpec((1, 1, m, k), lambda i: (0, i, 0, 0)),
            pl.BlockSpec((1, 1, k, m), lambda i: (0, i, 0, 0)),
        ],
        out_specs=[pl.BlockSpec((1, m, m), lambda i: (i, 0, 0))] * 2,
        cost_estimate=pl.CostEstimate(
            flops=4 * slots * m * k * m, bytes_accessed=6 * slots * m * k, transcendentals=0
        ),
        compiler_params=pltpu.CompilerParams(vmem_limit_bytes=24 << 20),
        name="edge_proj",
    )(edge, bedge, proj)


def product(left, right):
    return jnp.einsum("jmn,jnk->jmk", left, right, preferred_element_type=jnp.float32)


def per_device(corner, bcorner, edge, bedge, proj, joining, momentum):
    _, per_dev, m, _ = corner.shape
    blks = lax.axis_size("blk")
    sites = lax.axis_size("site")
    rows = m // blks
    my_site = lax.axis_index("site")
    left_corner, left_bcorner = shifted((corner, bcorner), "site", 1)
    w, v = edge_proj(edge, bedge, proj)
    angle = momentum[0] * my_site.astype(jnp.float32)
    cosine = jnp.cos(angle)
    sine = jnp.sin(angle)
    ground = product(left_corner[0], w).astype(jnp.bfloat16)
    real_term = product(left_bcorner[0, 0], w)
    imag_term = product(left_bcorner[1, 0], w)
    inserted = product(left_corner[0], v)
    re = (cosine * real_term - sine * imag_term + inserted).astype(jnp.bfloat16)
    im = (sine * real_term + cosine * imag_term).astype(jnp.bfloat16)
    local_peak = jnp.max(jnp.abs(ground))
    blocks = jnp.stack([ground, re, im], axis=1).reshape(per_dev, 3, blks, rows, m)
    blocks = jnp.moveaxis(blocks, 2, 0).reshape(blks, per_dev * 3 * rows, m)
    payload = jnp.concatenate([blocks, jnp.full((blks, 16, m), local_peak, jnp.bfloat16)], axis=1)
    arrived = lax.all_to_all(payload, "blk", 0, 0, tiled=True)
    peak = jnp.max(arrived[:, -16:].astype(jnp.float32))
    pieces = arrived[:, :-16].reshape(blks * per_dev, 3, rows, m)
    routed = pieces[joining[0]].astype(jnp.float32) / (peak + epsilon)
    scaled = routed.astype(jnp.bfloat16).reshape(blks, per_dev, 3, rows, m)
    final = lax.all_to_all(scaled, "blk", 0, 0, tiled=True)
    new = jnp.transpose(final, (2, 1, 0, 3, 4)).reshape(3, per_dev, m, m)
    terms = lax.all_to_all(final[:, :, 1:], "site", 0, 0, tiled=True)
    summed = jnp.sum(terms.reshape(sites, blks // sites, per_dev, 2, rows, m).astype(jnp.float32), axis=0)
    summed = jnp.transpose(summed, (2, 1, 0, 3, 4)).reshape(2, per_dev, m // sites, m)
    return (new[0][None], new[1:][:, None], summed)


def solution(mesh):
    in_specs = (
        P("site", "blk", None, None),
        P(None, "site", "blk", None, None),
        P("site", "blk", None, None),
        P("site", "blk", None, None),
        P("site", "blk", None, None),
        P("site", None),
        P(),
    )
    out_specs = (
        P("site", "blk", None, None),
        P(None, "site", "blk", None, None),
        P(None, "blk", "site", None),
    )
    return jax.shard_map(
        per_device, mesh=mesh, in_specs=in_specs, out_specs=out_specs, check_vma=False
    )
```

time: 172 us -> 74.3 us (0.43)
  waiting for transfers between devices: 86.1 us -> 22.7 us
  matrix products: 28.8 us -> 1.41 us
  between operations: 16.2 us -> 2.23 us
  starting transfers between devices: 3.21 us -> 12.4 us
  blocking collectives: 23.6 us -> 20.1 us
  other arithmetic: 4.23 us -> 0.87 us
  Pallas kernels: 0 us -> 2.79 us
    all_gather x1 -> x0, waiting for transfers between devices: 57.8 us -> none  [per_device(): piece = lax.all_gather(projected, 'blk', axis=0, tiled=True)]
    unnamed x3 -> x0, waiting for transfers between devices: 26.1 us -> none
    pmax x1 -> x0, blocking collectives: 23.6 us -> none  [per_device(): peak = lax.pmax(local_peak, 'blk')]
    all_to_all x0 -> x2, waiting for transfers between devices: none -> 22.7 us  [the longest x1 16.8 us: per_device(): arrived = lax.all_to_all(payload, 'blk', 0, 0, tiled=True)]
    dot_general x5 -> x4, matrix products: 23.8 us -> 1.41 us  [product(): jnp.einsum('jmn,jnk->jmk', left, right, preferred_element_type=jnp.float32)]
    all_to_all x0 -> x1, blocking collectives: none -> 20.1 us  [per_device(): final = lax.all_to_all(scaled, 'blk', 0, 0, tiled=True)]
    all_to_all x0 -> x2, starting transfers between devices: none -> 9.26 us  [the longest x1 5.8 us: per_device(): arrived = lax.all_to_all(payload, 'blk', 0, 0, tiled=True)]
    dot_general x1 -> x0, matrix products: 5.01 us -> none  [per_device(): jnp.einsum('it,txmn->ixmn', picks, piece, preferred_element_type=jnp.floa...]
  transfers between devices with their start and end apart: 4 -> 4, of which waited for: 3 -> 2; matrix products, arithmetic and copies ran while one was open for 6% -> 3% of each run, Pallas kernels for 0% -> 4%
where the time goes in v1:
time: 74.3 us; the launch traced here: 73.8 us
  waiting for transfers between devices  22.7 us (31%)
  blocking collectives  20.1 us (27%)
  starting transfers between devices  12.4 us (17%)
  local copies, waits for them, and re-layouts  11.3 us (15%)
  Pallas kernels  2.79 us (4%)
  between operations  2.23 us (3%)
  matrix products  1.41 us (2%)
  other arithmetic  0.87 us (1%)
    all_to_all x1, blocking collectives, per_device(): final = lax.all_to_all(scaled, 'blk', 0, 0, tiled=True)  20.1 us
    all_to_all x1, waiting for transfers between devices, per_device(): arrived = lax.all_to_all(payload, 'blk', 0, 0, tiled=True)  16.8 us
    unnamed x8, local copies, waits for them, and re-layouts  6 us
    all_to_all x1, waiting for transfers between devices, per_device(): terms = lax.all_to_all(final[:, :, 1:], 'site', 0, 0, tiled=True)  5.88 us
    all_to_all x1, starting transfers between devices, per_device(): arrived = lax.all_to_all(payload, 'blk', 0, 0, tiled=True)  5.8 us
    all_to_all x1, starting transfers between devices, per_device(): terms = lax.all_to_all(final[:, :, 1:], 'site', 0, 0, tiled=True)  3.46 us
    ppermute x2, starting transfers between devices, shifted(): return lax.ppermute(block, axis, route)  3.13 us
    pallas_call x1, Pallas kernels, edge_proj(): pl.pallas_call(edge_proj_kernel, grid=(slots,), out_shape=(block, block),...  2.79 us
  transfers between devices with their start and end apart: 4, of which 2 were waited for; matrix products, arithmetic and copies ran while one was open for 3% of the time, Pallas kernels for 4%

profile of v1, /device:TPU:0, one launch (start us, length us, event | category | flops | bytes accessed | tf_op | source)
XLA Modules:
  0.0 73.8 jit_solution(16227593536769644359)
XLA Ops:
  0.6 0.5 collective-permute-start
  1.1 2.6 %collective-permute-start.1 = (bf16[2,1,6,128,128]{4,3,2,1,0:T(8,128)(2,1)}, bf16[2,1,6,128,128]{4,3,2,1,0:T(8,128)(2,1)S(1)}, u32[]{:S(2)}, u32[]{:S(2)}) collective-permute-start(bf16[2,1,6,128,128]{4,3,2,1,0:T(8,128)(2,1)} %param.8), channel_id=1, source_target_pairs={{24,0},{0,8},{8,16},{16,24},{25,1},{1,9},{9,17},{17,25},{26,2},{2,... | collective-permute-start | bytes 1179656 | tf_op jit(solution)/shard_map/ppermute | solution.py:14
  4.6 0.0 copy-start
  4.6 2.0 %copy-done = bf16[1,6,128,2304]{3,2,1,0:T(8,128)(2,1)S(1)} copy-done((bf16[1,6,128,2304]{3,2,1,0:T(8,128)(2,1)S(1)}, bf16[1,6,128,2304]{3,2,1,0:T(8,128)(2,1)}, u32[]{:S(2)}) %copy-start) | copy-done | bytes 3538968
  6.6 0.0 copy-start.1
  6.6 2.0 %copy-done.1 = bf16[1,6,128,2304]{3,2,1,0:T(8,128)(2,1)S(1)} copy-done((bf16[1,6,128,2304]{3,2,1,0:T(8,128)(2,1)S(1)}, bf16[1,6,128,2304]{3,2,1,0:T(8,128)(2,1)}, u32[]{:S(2)}) %copy-start.1) | copy-done | bytes 3538968
  8.6 0.0 copy-start.2
  8.6 2.0 %copy-done.2 = bf16[1,6,2304,128]{3,2,1,0:T(8,128)(2,1)S(1)} copy-done((bf16[1,6,2304,128]{3,2,1,0:T(8,128)(2,1)S(1)}, bf16[1,6,2304,128]{3,2,1,0:T(8,128)(2,1)}, u32[]{:S(2)}) %copy-start.2) | copy-done | bytes 3538968
  10.6 2.8 %edge_proj.1 = (bf16[6,128,128]{2,1,0:T(8,128)(2,1)S(1)}, bf16[6,128,128]{2,1,0:T(8,128)(2,1)S(1)}) custom-call(bf16[1,6,128,2304]{3,2,1,0:T(8,128)(2,1)S(1)} %copy-done, bf16[1,6,128,2304]{3,2,1,0:T(8,128)(2,1)S(1)} %copy-done.1, bf16[1,6,2304,128]{3,2,1,0:T(8,128)(2,1)S(1)} %copy-done.2), custom_call_target="tpu_custom_call" | custom-call | flops 905969664 | bytes 10616832 | tf_op jit(solution)/shard_map/edge_proj/pallas_call | solution.py:26
  13.4 0.0 collective-permute-done
  13.4 0.8 %fusion.2 = (bf16[]{:T(256)}, bf16[6,128,128]{1,2,0:T(8,128)(2,1)S(1)}) fusion(bf16[6,128,128]{2,1,0:T(8,128)(2,1)S(1)} %get-tuple-element.5, bf16[1,6,128,128]{3,2,1,0:T(8,128)(2,1)S(1)} %collective-permute-done), kind=kOutput, calls=%fused_computation.12 | convolution fusion | flops 25460736 | bytes 589826 | tf_op jit(solution)/shard_map/jmn,jnk->jmk/dot_general | solution.py:45
  14.2 0.0 collective-permute-done.1
  14.2 0.2 fusion.1
  14.4 0.0 copy-start.3
  14.4 0.2 add_convert_fusion
  14.6 0.2 add_convert_fusion.1
  14.8 0.1 pad_maximum_fusion
  14.9 0.1 copy.32
  15.0 1.5 %concatenate.4 = bf16[8,304,128]{2,1,0:T(8,128)(2,1)} pad(bf16[8,288,128]{2,1,0:T(8,128)(2,1)S(1)} %bitcast.55, bf16[]{:T(256)} %get-tuple-element.18), padding=0_0x0_16x0_0 | pad | bytes 1212418 | tf_op jit(solution)/shard_map/concatenate | solution.py:68
  16.5 5.8 %all-to-all-start = ((bf16[8,304,128]{2,1,0:T(8,128)(2,1)}), bf16[8,304,128]{2,1,0:T(8,128)(2,1)S(1)}, u32[]{:S(2)}, u32[]{:S(2)}) async-start(bf16[8,304,128]{2,1,0:T(8,128)(2,1)} %concatenate.4), calls=%async_computation | async-start | bytes 1245184 | tf_op jit(solution)/shard_map/all_to_all | solution.py:69
  22.4 0.0 copy-done.3
  22.4 16.8 %all-to-all-done = bf16[8,304,128]{2,1,0:T(8,128)(2,1)S(1)} async-done(((bf16[8,304,128]{2,1,0:T(8,128)(2,1)}), bf16[8,304,128]{2,1,0:T(8,128)(2,1)S(1)}, u32[]{:S(2)}, u32[]{:S(2)}) %all-to-all-start) | async-done | bytes 622624 | tf_op jit(solution)/shard_map/all_to_all | solution.py:69
  39.2 0.7 gather_fusion
  39.9 0.6 slice_reduce_fusion
  41.2 0.1 divide_convert_fusion
  41.3 20.1 %all_to_all.15 = bf16[8,6,3,16,128]{4,3,2,1,0:T(8,128)(2,1)S(1)} all-to-all(bf16[8,6,3,16,128]{4,3,2,1,0:T(8,128)(2,1)S(1)} %bitcast.56), channel_id=1, replica_groups=mesh['site'=4,'blk'=8] {'blk'}, dimensions={0} | all-to-all | bytes 1179648 | tf_op jit(solution)/shard_map/all_to_all | solution.py:74
  61.4 0.8 %slice.41 = bf16[8,6,2,16,128]{4,3,2,1,0:T(8,128)(2,1)} slice(bf16[8,6,3,16,128]{4,3,2,1,0:T(8,128)(2,1)S(1)} %all_to_all.15), slice={[0:8], [0:6], [1:3], [0:16], [0:128]} | slice | bytes 786432 | tf_op jit(solution)/shard_map/slice | solution.py:76
  62.2 3.5 %all-to-all-start.2 = ((bf16[8,6,2,16,128]{4,3,2,1,0:T(8,128)(2,1)}), bf16[8,6,2,16,128]{4,3,2,1,0:T(8,128)(2,1)S(1)}, u32[]{:S(2)}, u32[]{:S(2)}) async-start(bf16[8,6,2,16,128]{4,3,2,1,0:T(8,128)(2,1)} %slice.41), calls=%async_computation.2 | async-start | bytes 786432 | tf_op jit(solution)/shard_map/all_to_all | solution.py:76
  65.7 0.8 %copy.29 = bf16[2,6,8,16,128]{4,3,2,1,0:T(8,128)(2,1)} copy(bf16[2,6,8,16,128]{4,3,0,1,2:T(8,128)(2,1)S(1)} %slice.40) | data formatting | bytes 786432 | tf_op jit(solution)/shard_map/slice | solution.py:79
  66.5 0.7 copy.28
  67.2 5.9 %all-to-all-done.2 = bf16[8,6,2,16,128]{4,3,2,1,0:T(8,128)(2,1)S(1)} async-done(((bf16[8,6,2,16,128]{4,3,2,1,0:T(8,128)(2,1)}), bf16[8,6,2,16,128]{4,3,2,1,0:T(8,128)(2,1)S(1)}, u32[]{:S(2)}, u32[]{:S(2)}) %all-to-all-start.2) | async-done | bytes 393248 | tf_op jit(solution)/shard_map/all_to_all | solution.py:76
  73.1 0.1 convert_reduce_fusion
  73.1 0.7 copy.30
  (5 shorter events, 0.1 us)
Async XLA Ops:
  0.6 12.8 %collective-permute-start = (bf16[1,6,128,128]{3,2,1,0:T(8,128)(2,1)}, bf16[1,6,128,128]{3,2,1,0:T(8,128)(2,1)S(1)}, u32[]{:S(2)}, u32[]{:S(2)}) collective-permute-start(bf16[1,6,128,128]{3,2,1,0:T(8,128)(2,1)} %param.7), channel_id=1, source_target_pairs={{24,0},{0,8},{8,16},{16,24},{25,1},{1,9},{9,17},{17,25},{26,2},{2,... | collective-permute-start | bytes 589832 | tf_op jit(solution)/shard_map/ppermute | solution.py:14
  1.1 13.1 %collective-permute-start.1 = (bf16[2,1,6,128,128]{4,3,2,1,0:T(8,128)(2,1)}, bf16[2,1,6,128,128]{4,3,2,1,0:T(8,128)(2,1)S(1)}, u32[]{:S(2)}, u32[]{:S(2)}) collective-permute-start(bf16[2,1,6,128,128]{4,3,2,1,0:T(8,128)(2,1)} %param.8), channel_id=1, source_target_pairs={{24,0},{0,8},{8,16},{16,24},{25,1},{1,9},{9,17},{17,25},{26,2},{2,... | collective-permute-start | bytes 1179656 | tf_op jit(solution)/shard_map/ppermute | solution.py:14
  4.6 2.0 %copy-start = (bf16[1,6,128,2304]{3,2,1,0:T(8,128)(2,1)S(1)}, bf16[1,6,128,2304]{3,2,1,0:T(8,128)(2,1)}, u32[]{:S(2)}) copy-start(bf16[1,6,128,2304]{3,2,1,0:T(8,128)(2,1)} %edge_ref.1) | copy-start | bytes 10616836
  6.6 2.0 %copy-start.1 = (bf16[1,6,128,2304]{3,2,1,0:T(8,128)(2,1)S(1)}, bf16[1,6,128,2304]{3,2,1,0:T(8,128)(2,1)}, u32[]{:S(2)}) copy-start(bf16[1,6,128,2304]{3,2,1,0:T(8,128)(2,1)} %bedge_ref.1) | copy-start | bytes 10616836
  8.6 2.0 %copy-start.2 = (bf16[1,6,2304,128]{3,2,1,0:T(8,128)(2,1)S(1)}, bf16[1,6,2304,128]{3,2,1,0:T(8,128)(2,1)}, u32[]{:S(2)}) copy-start(bf16[1,6,2304,128]{3,2,1,0:T(8,128)(2,1)} %proj_ref.1) | copy-start | bytes 10616836
  14.4 8.0 %copy-start.3 = (s32[1,48]{1,0:T(1,128)S(1)}, s32[1,48]{1,0:T(1,128)}, u32[]{:S(2)}) copy-start(s32[1,48]{1,0:T(1,128)} %param.12) | copy-start | bytes 580
  16.5 22.6 %all-to-all-start = ((bf16[8,304,128]{2,1,0:T(8,128)(2,1)}), bf16[8,304,128]{2,1,0:T(8,128)(2,1)S(1)}, u32[]{:S(2)}, u32[]{:S(2)}) async-start(bf16[8,304,128]{2,1,0:T(8,128)(2,1)} %concatenate.4), calls=%async_computation | async-start | bytes 1245184 | tf_op jit(solution)/shard_map/all_to_all | solution.py:69
  62.2 10.9 %all-to-all-start.2 = ((bf16[8,6,2,16,128]{4,3,2,1,0:T(8,128)(2,1)}), bf16[8,6,2,16,128]{4,3,2,1,0:T(8,128)(2,1)S(1)}, u32[]{:S(2)}, u32[]{:S(2)}) async-start(bf16[8,6,2,16,128]{4,3,2,1,0:T(8,128)(2,1)} %slice.41), calls=%async_computation.2 | async-start | bytes 786432 | tf_op jit(solution)/shard_map/all_to_all | solution.py:76

commit v2 on v1

v2 whole, which is shorter than its diff:
```python
import functools

import jax
import jax.numpy as jnp
from jax import lax
from jax.experimental import pallas as pl
from jax.experimental.pallas import tpu as pltpu
from jax.sharding import PartitionSpec as P

epsilon = 1e-06
CAP = 2
TILE = 16
VMEM = pl.BlockSpec(memory_space=pltpu.VMEM)
SMEM = pl.BlockSpec(memory_space=pltpu.SMEM)
HBM = pl.BlockSpec(memory_space=pltpu.HBM)


def swapped(part, axis, k):
    n = lax.axis_size(axis)
    return part if k == 0 else lax.ppermute(part, axis, [(i, i ^ k) for i in range(n)])


def all_swapped(parts, axis):
    order = sorted(range(len(parts)), reverse=True)
    out = {k: swapped(parts[k], axis, k) for k in order}
    return [out[k] for k in range(len(parts))]


def edge_proj_kernel(edge, bedge, proj, w_ref, v_ref, edge_buf, bedge_buf, proj_buf, sems):
    slots = w_ref.shape[0]
    pairs = ((proj, proj_buf), (edge, edge_buf), (bedge, bedge_buf))
    copies = [
        [pltpu.make_async_copy(src.at[0, i], buf.at[i], sems.at[3 * i + a]) for a, (src, buf) in enumerate(pairs)]
        for i in range(slots)
    ]
    for group in copies:
        for copy in group:
            copy.start()
    dot = functools.partial(jnp.dot, preferred_element_type=jnp.float32)
    for i, (first, second, third) in enumerate(copies):
        first.wait()
        second.wait()
        w_ref[i] = dot(edge_buf[i], proj_buf[i]).astype(w_ref.dtype)
        third.wait()
        v_ref[i] = dot(bedge_buf[i], proj_buf[i]).astype(v_ref.dtype)


def edge_proj(edge, bedge, proj):
    _, slots, m, k = edge.shape
    block = jax.ShapeDtypeStruct((slots, m, m), jnp.bfloat16)
    return pl.pallas_call(
        edge_proj_kernel,
        out_shape=(block, block),
        in_specs=[HBM] * 3,
        out_specs=[VMEM] * 2,
        scratch_shapes=[
            pltpu.VMEM((slots, m, k), jnp.bfloat16),
            pltpu.VMEM((slots, m, k), jnp.bfloat16),
            pltpu.VMEM((slots, k, m), jnp.bfloat16),
            pltpu.SemaphoreType.DMA((3 * slots,)),
        ],
        cost_estimate=pl.CostEstimate(
            flops=4 * slots * m * k * m, bytes_accessed=6 * slots * m * k, transcendentals=0
        ),
        compiler_params=pltpu.CompilerParams(vmem_limit_bytes=20 << 20),
        name="edge_proj",
    )(edge, bedge, proj)


def small_call(kernel, out_shape, in_specs, scratch, name):
    return pl.pallas_call(
        kernel,
        out_shape=out_shape,
        in_specs=in_specs,
        out_specs=jax.tree.map(lambda _: VMEM, out_shape),
        scratch_shapes=scratch,
        cost_estimate=pl.CostEstimate(flops=1 << 28, bytes_accessed=1 << 20, transcendentals=0),
        compiler_params=pltpu.CompilerParams(vmem_limit_bytes=24 << 20),
        name=name,
    )


def project_kernel(n, here, turn, joining, corner, bcorner, w, v, *refs):
    b_out, g_out, stage, picks = refs[:n], refs[n : 2 * n], refs[2 * n], refs[2 * n + 1]
    slots, m, _ = w.shape
    me, cosine, sine = here[0], turn[0], turn[1]
    dot = functools.partial(jnp.dot, preferred_element_type=jnp.float32)
    top = jnp.zeros((m, m), jnp.float32)
    for i in range(slots):
        ground = dot(corner[0, i], w[i]).astype(jnp.bfloat16)
        real_term = dot(bcorner[0, 0, i], w[i])
        imag_term = dot(bcorner[1, 0, i], w[i])
        re = cosine * real_term - sine * imag_term + dot(corner[0, i], v[i])
        im = sine * real_term + cosine * imag_term
        stage[3 * i] = ground
        stage[3 * i + 1] = re.astype(jnp.bfloat16)
        stage[3 * i + 2] = im.astype(jnp.bfloat16)
        top = jnp.maximum(top, jnp.abs(ground.astype(jnp.float32)))
    peak = jnp.full((TILE, m), jnp.max(top), jnp.float32).astype(jnp.bfloat16)
    for p in range(CAP * n):
        picks[p] = 0
    for t in range(n):
        count = jnp.int32(0)
        for i in range(slots):
            mine = joining[0, t * slots + i] - me * slots
            inside = jnp.logical_and(mine >= 0, mine < slots)
            picks[jnp.where(inside, CAP * t + count, CAP * n)] = mine
            count = count + inside.astype(jnp.int32)
    for k in range(n):
        t = jnp.bitwise_xor(me, k)
        for j in range(CAP):
            slot = picks[CAP * t + j]
            g_out[k][j * m : (j + 1) * m] = stage[3 * slot]
            for c in range(2):
                at = (2 * j + c) * m
                b_out[k][at : at + m] = stage[3 * slot + 1 + c]
        b_out[k][2 * CAP * m :] = peak


def project(here, turn, joining, corner, bcorner, w, v, n):
    slots, m, _ = w.shape
    b_piece = jax.ShapeDtypeStruct((2 * CAP * m + TILE, m), jnp.bfloat16)
    g_piece = jax.ShapeDtypeStruct((CAP * m, m), jnp.bfloat16)
    out = small_call(
        functools.partial(project_kernel, n),
        [b_piece] * n + [g_piece] * n,
        [SMEM] * 3 + [VMEM] * 4,
        [pltpu.VMEM((3 * slots, m, m), jnp.bfloat16), pltpu.SMEM((CAP * n + 1,), jnp.int32)],
        "project",
    )(here, turn, joining, corner, bcorner, w, v)
    return out[:n], out[n:]


def find_places(n, slots, me, joining, places):
    for p in range(CAP * n):
        places[p] = -1
    owners = []
    for i in range(slots):
        owner = lax.div(joining[0, me * slots + i], slots)
        rank = sum([(other == owner).astype(jnp.int32) for other in owners], jnp.int32(0))
        places[CAP * owner + rank] = i
        owners.append(owner)


def join_b_kernel(n, shared, here, joining, *refs):
    pieces, new, peak, shares, places = refs[:n], refs[n], refs[n + 1], refs[n + 2 : -1], refs[-1]
    _, _, slots, m, _ = new.shape
    find_places(n, slots, here[0], joining, places)
    top = pieces[0][2 * CAP * m :].astype(jnp.float32)
    for k in range(1, n):
        top = jnp.maximum(top, pieces[k][2 * CAP * m :].astype(jnp.float32))
    peak[...] = top
    divisor = jnp.concatenate([top] * (m // TILE), axis=0) + epsilon
    for k in range(n):
        d = jnp.bitwise_xor(here[0], k)
        for j in range(CAP):
            place = places[CAP * d + j]

            @pl.when(place >= 0)
            def _():
                for c in range(2):
                    at = (2 * j + c) * m
                    new[c, 0, place] = (pieces[k][at : at + m].astype(jnp.float32) / divisor).astype(jnp.bfloat16)

    for k in range(shared):
        wide = m // shared
        first = pl.multiple_of(jnp.bitwise_xor(here[1], k) * wide, wide)
        for i in range(slots):
            for c in range(2):
                shares[k][c, i] = new[c, 0, i, pl.ds(first, wide)]


def join_b(here, joining, pieces, slots, m, shared):
    n = len(pieces)
    share = [jax.ShapeDtypeStruct((2, slots, m // shared, m), jnp.bfloat16)] * shared if shared else []
    return small_call(
        functools.partial(join_b_kernel, n, shared),
        [jax.ShapeDtypeStruct((2, 1, slots, m, m), jnp.bfloat16), jax.ShapeDtypeStruct((TILE, m), jnp.float32)] + share,
        [SMEM] * 2 + [VMEM] * n,
        [pltpu.SMEM((CAP * n,), jnp.int32)],
        "join_b",
    )(here, joining, *pieces)


def join_g_kernel(n, here, joining, peak, *refs):
    pieces, new, places = refs[:n], refs[n], refs[n + 1]
    _, slots, m, _ = new.shape
    find_places(n, slots, here[0], joining, places)
    divisor = jnp.concatenate([peak[...]] * (m // TILE), axis=0) + epsilon
    for k in range(n):
        d = jnp.bitwise_xor(here[0], k)
        for j in range(CAP):
            place = places[CAP * d + j]

            @pl.when(place >= 0)
            def _():
                piece = pieces[k][j * m : (j + 1) * m].astype(jnp.float32)
                new[0, place] = (piece / divisor).astype(jnp.bfloat16)


def join_g(here, joining, peak, pieces, slots, m):
    n = len(pieces)
    return small_call(
        functools.partial(join_g_kernel, n),
        [jax.ShapeDtypeStruct((1, slots, m, m), jnp.bfloat16)],
        [SMEM] * 2 + [VMEM] * (n + 1),
        [pltpu.SMEM((CAP * n,), jnp.int32)],
        "join_g",
    )(here, joining, peak, *pieces)[0]


def per_device(corner, bcorner, edge, bedge, proj, joining, momentum):
    _, slots, m, _ = corner.shape
    n, sites = lax.axis_size("blk"), lax.axis_size("site")
    my_site = lax.axis_index("site")
    here = jnp.stack([lax.axis_index("blk"), my_site]).astype(jnp.int32)
    angle = momentum[0] * my_site.astype(jnp.float32)
    turn = jnp.stack([jnp.cos(angle), jnp.sin(angle)])
    onward = [(i, (i + 1) % sites) for i in range(sites)]
    left_corner = lax.ppermute(corner, "site", onward)
    left_bcorner = lax.ppermute(bcorner, "site", onward)
    w, v = edge_proj(edge, bedge, proj)
    b_parts, g_parts = project(here, turn, joining, left_corner, left_bcorner, w, v, n)
    b_parts = all_swapped(b_parts, "blk")
    g_parts = all_swapped(g_parts, "blk")
    shared = sites if m % (sites * TILE) == 0 else 0
    new_b, peak, *shares = join_b(here, joining, b_parts, slots, m, shared)
    if shared:
        shares = all_swapped(shares, "site")
    else:
        shares = jnp.moveaxis(new_b.reshape(2, slots, sites, m // sites, m), 2, 0)
        shares = lax.all_to_all(shares, "site", 0, 0, tiled=True)
    new_corner = join_g(here, joining, peak, g_parts, slots, m)
    summed = shares[0].astype(jnp.float32)
    for k in range(1, sites):
        summed = summed + shares[k].astype(jnp.float32)
    return (new_corner, new_b, summed)


def solution(mesh):
    in_specs = (
        P("site", "blk", None, None),
        P(None, "site", "blk", None, None),
        P("site", "blk", None, None),
        P("site", "blk", None, None),
        P("site", "blk", None, None),
        P("site", None),
        P(),
    )
    out_specs = (
        P("site", "blk", None, None),
        P(None, "site", "blk", None, None),
        P(None, "blk", "site", None),
    )
    return jax.shard_map(
        per_device, mesh=mesh, in_specs=in_specs, out_specs=out_specs, check_vma=False
    )
```

time: 74.3 us -> 67.6 us (0.910)
  starting transfers between devices: 12.4 us -> 40.1 us
  blocking collectives: 20.1 us -> 0 us
  waiting for transfers between devices: 22.7 us -> 8.63 us
  Pallas kernels: 2.79 us -> 10.3 us
  local copies, waits for them, and re-layouts: 11.3 us -> 6.01 us
  matrix products: 1.41 us -> 0 us
    ppermute x2 -> x19, starting transfers between devices: 3.13 us -> 40.1 us  [the longest x17 37 us: swapped(): lax.ppermute(part, axis, [(i, i ^ k) for i in range(n)])]
    all_to_all x2 -> x0, waiting for transfers between devices: 22.7 us -> none  [the longest x1 16.8 us: per_device(): arrived = lax.all_to_all(payload, 'blk', 0, 0, tiled=True)]
    all_to_all x1 -> x0, blocking collectives: 20.1 us -> none  [per_device(): final = lax.all_to_all(scaled, 'blk', 0, 0, tiled=True)]
    all_to_all x2 -> x0, starting transfers between devices: 9.26 us -> none  [the longest x1 5.8 us: per_device(): arrived = lax.all_to_all(payload, 'blk', 0, 0, tiled=True)]
    ppermute x2 -> x19, waiting for transfers between devices: 0.01 us -> 8.63 us  [the longest x17 8.62 us: swapped(): lax.ppermute(part, axis, [(i, i ^ k) for i in range(n)])]
    pallas_call x1 -> x4, Pallas kernels: 2.79 us -> 10.3 us  [the longest x1 6.19 us: edge_proj(): pl.pallas_call(edge_proj_kernel, out_shape=(block, block), in_specs=[HBM]...]
    slice x6 -> x0, local copies, waits for them, and re-layouts: 2.33 us -> none  [the longest x4 1.51 us: per_device(): return (new[0][None], new[1:][:, None], summed)]
    concatenate x1 -> x0, local copies, waits for them, and re-layouts: 1.52 us -> none  [per_device(): jnp.concatenate([blocks, jnp.full((blks, 16, m), local_peak, jnp.bfloat16...]
  transfers between devices with their start and end apart: 4 -> 19, of which waited for: 2 -> 5; matrix products, arithmetic and copies ran while one was open for 3% -> 0% of each run, Pallas kernels for 4% -> 14%
where the time goes in v2:
time: 67.6 us; the launch traced here: 67.4 us
  starting transfers between devices  40.1 us (59%)
  Pallas kernels  10.3 us (15%)
  waiting for transfers between devices  8.63 us (13%)
  local copies, waits for them, and re-layouts  6.01 us (9%)
  between operations  1.49 us (2%)
  other arithmetic  0.88 us (1%)
    ppermute x17, starting transfers between devices, swapped(): lax.ppermute(part, axis, [(i, i ^ k) for i in range(n)])  37 us
    ppermute x17, waiting for transfers between devices, swapped(): lax.ppermute(part, axis, [(i, i ^ k) for i in range(n)])  8.62 us
    pallas_call x1, Pallas kernels, edge_proj(): pl.pallas_call(edge_proj_kernel, out_shape=(block, block), in_specs=[HBM]...  6.19 us
    unnamed x8, local copies, waits for them, and re-layouts  6.01 us
    ppermute x1, starting transfers between devices, per_device(): left_corner = lax.ppermute(corner, 'site', onward)  2.63 us
    pallas_call x1, Pallas kernels, join_b(): small_call(functools.partial(join_b_kernel, n, shared), [jax.ShapeDtypeSt...  1.56 us
    pallas_call x1, Pallas kernels, join_g(): small_call(functools.partial(join_g_kernel, n), [jax.ShapeDtypeStruct((1,...  1.47 us
  transfers between devices with their start and end apart: 19, of which 5 were waited for; matrix products, arithmetic and copies ran while one was open for 0% of the time, Pallas kernels for 14%

profile of v2, /device:TPU:0, one launch (start us, length us, event | category | flops | bytes accessed | tf_op | source)
XLA Modules:
  0.0 67.4 jit_solution(2723142990712499749)
XLA Ops:
  0.6 0.5 collective-permute-start.1
  1.1 2.6 %collective-permute-start = (bf16[1,6,128,128]{3,2,1,0:T(8,128)(2,1)}, bf16[1,6,128,128]{3,2,1,0:T(8,128)(2,1)S(1)}, u32[]{:S(2)}, u32[]{:S(2)}) collective-permute-start(bf16[1,6,128,128]{3,2,1,0:T(8,128)(2,1)} %param.7), channel_id=1, source_target_pairs={{0,8},{8,16},{16,24},{24,0},{1,9},{9,17},{17,25},{25,1},{2,10},{10... | collective-permute-start | bytes 589832 | tf_op jit(solution)/shard_map/ppermute | solution.py:220
  4.6 0.1 pad_add_fusion.here
  4.6 2.0 %copy-done = bf16[1,6,128,2304]{3,2,1,0:T(8,128)(2,1)S(1)} copy-done((bf16[1,6,128,2304]{3,2,1,0:T(8,128)(2,1)S(1)}, bf16[1,6,128,2304]{3,2,1,0:T(8,128)(2,1)}, u32[]{:S(2)}) %copy-start) | copy-done | bytes 3538968
  6.7 2.0 %copy-done.1 = bf16[1,6,128,2304]{3,2,1,0:T(8,128)(2,1)S(1)} copy-done((bf16[1,6,128,2304]{3,2,1,0:T(8,128)(2,1)S(1)}, bf16[1,6,128,2304]{3,2,1,0:T(8,128)(2,1)}, u32[]{:S(2)}) %copy-start.1) | copy-done | bytes 3538968
  8.7 2.0 %copy-done.2 = bf16[1,6,2304,128]{3,2,1,0:T(8,128)(2,1)S(1)} copy-done((bf16[1,6,2304,128]{3,2,1,0:T(8,128)(2,1)S(1)}, bf16[1,6,2304,128]{3,2,1,0:T(8,128)(2,1)}, u32[]{:S(2)}) %copy-start.2) | copy-done | bytes 3538968
  10.7 6.2 %edge_proj.1 = (bf16[6,128,128]{2,1,0:T(8,128)(2,1)S(1)}, bf16[6,128,128]{2,1,0:T(8,128)(2,1)S(1)}) custom-call(bf16[1,6,128,2304]{3,2,1,0:T(8,128)(2,1)S(1)} %copy-done, bf16[1,6,128,2304]{3,2,1,0:T(8,128)(2,1)S(1)} %copy-done.1, bf16[1,6,2304,128]{3,2,1,0:T(8,128)(2,1)S(1)} %copy-done.2), custom_call_target="tpu_custom_call" | custom-call | flops 905969664 | bytes 10616832 | tf_op jit(solution)/shard_map/edge_proj/pallas_call | solution.py:51
  16.9 0.1 pad_maximum_fusion.turn
  16.9 0.0 collective-permute-done.corner
  16.9 0.0 collective-permute-done.1.bcorner
  16.9 1.1 %project.1 = (bf16[528,128]{1,0:T(8,128)(2,1)S(1)}, bf16[528,128]{1,0:T(8,128)(2,1)S(1)}, bf16[528,128]{1,0:T(8,128)(2,1)S(1)}, bf16[528,128]{1,0:T(8,128)(2,1)S...) custom-call(s32[2]{0:T(128)S(1)} %pad_add_fusion.here, ...), custom_call_target="tpu_custom_call" | custom-call | flops 268435456 | bytes 1048576 | tf_op jit(solution)/shard_map/project/pallas_call | solution.py:124
  18.0 1.6 %collective-permute-start.2 = (bf16[528,128]{1,0:T(8,128)(2,1)S(1)}, bf16[528,128]{1,0:T(8,128)(2,1)S(1)}, u32[]{:S(2)}, u32[]{:S(2)}) collective-permute-start(bf16[528,128]{1,0:T(8,128)(2,1)S(1)} %get-tuple-element.30), channel_id=1, source_target_pairs={{0,1},{1,0},{2,3},{3,2},{4,5},{5,4},{6,7},{7,6},{8,9},{9,8},{10,11... | collective-permute-start | bytes 405512 | tf_op jit(solution)/shard_map/ppermute | solution.py:20
  19.6 1.6 %collective-permute-start.3 = (bf16[528,128]{1,0:T(8,128)(2,1)S(1)}, bf16[528,128]{1,0:T(8,128)(2,1)S(1)}, u32[]{:S(2)}, u32[]{:S(2)}) collective-permute-start(bf16[528,128]{1,0:T(8,128)(2,1)S(1)} %get-tuple-element.31), channel_id=1, source_target_pairs={{0,2},{1,3},{2,0},{3,1},{4,6},{5,7},{6,4},{7,5},{8,10},{9,11},{10,... | collective-permute-start | bytes 405512 | tf_op jit(solution)/shard_map/ppermute | solution.py:20
  21.2 0.4 collective-permute-start.4
  21.6 2.6 %collective-permute-start.5 = (bf16[528,128]{1,0:T(8,128)(2,1)S(1)}, bf16[528,128]{1,0:T(8,128)(2,1)S(1)}, u32[]{:S(2)}, u32[]{:S(2)}) collective-permute-start(bf16[528,128]{1,0:T(8,128)(2,1)S(1)} %get-tuple-element.33), channel_id=1, source_target_pairs={{0,4},{1,5},{2,6},{3,7},{4,0},{5,1},{6,2},{7,3},{8,12},{9,13},{10,... | collective-permute-start | bytes 405512 | tf_op jit(solution)/shard_map/ppermute | solution.py:20
  24.2 1.3 %collective-permute-start.6 = (bf16[528,128]{1,0:T(8,128)(2,1)S(1)}, bf16[528,128]{1,0:T(8,128)(2,1)S(1)}, u32[]{:S(2)}, u32[]{:S(2)}) collective-permute-start(bf16[528,128]{1,0:T(8,128)(2,1)S(1)} %get-tuple-element.34), channel_id=1, source_target_pairs={{0,5},{1,4},{2,7},{3,6},{4,1},{5,0},{6,3},{7,2},{8,13},{9,12},{10,... | collective-permute-start | bytes 405512 | tf_op jit(solution)/shard_map/ppermute | solution.py:20
  25.4 0.0 collective-permute-done.2.refs_1_
  25.4 3.6 %collective-permute-start.7 = (bf16[528,128]{1,0:T(8,128)(2,1)S(1)}, bf16[528,128]{1,0:T(8,128)(2,1)S(1)}, u32[]{:S(2)}, u32[]{:S(2)}) collective-permute-start(bf16[528,128]{1,0:T(8,128)(2,1)S(1)} %get-tuple-element.35), channel_id=1, source_target_pairs={{0,6},{1,7},{2,4},{3,5},{4,2},{5,3},{6,0},{7,1},{8,14},{9,15},{10,... | collective-permute-start | bytes 405512 | tf_op jit(solution)/shard_map/ppermute | solution.py:20
  29.0 1.6 %collective-permute-done.3.refs_2_ = bf16[528,128]{1,0:T(8,128)(2,1)S(1)} collective-permute-done((bf16[528,128]{1,0:T(8,128)(2,1)S(1)}, bf16[528,128]{1,0:T(8,128)(2,1)S(1)}, u32[]{:S(2)}, u32[]{:S(2)}) %collective-permute-start.3) | collective-permute-done | bytes 135200 | tf_op jit(solution)/shard_map/ppermute | solution.py:20
  30.6 0.8 %collective-permute-start.8 = (bf16[528,128]{1,0:T(8,128)(2,1)S(1)}, bf16[528,128]{1,0:T(8,128)(2,1)S(1)}, u32[]{:S(2)}, u32[]{:S(2)}) collective-permute-start(bf16[528,128]{1,0:T(8,128)(2,1)S(1)} %get-tuple-element.36), channel_id=1, source_target_pairs={{0,7},{1,6},{2,5},{3,4},{4,3},{5,2},{6,1},{7,0},{8,15},{9,14},{10,... | collective-permute-start | bytes 405512 | tf_op jit(solution)/shard_map/ppermute | solution.py:20
  31.4 0.7 collective-permute-done.4.refs_3_
  32.1 2.4 %collective-permute-start.9 = (bf16[256,128]{1,0:T(8,128)(2,1)S(1)}, bf16[256,128]{1,0:T(8,128)(2,1)S(1)}, u32[]{:S(2)}, u32[]{:S(2)}) collective-permute-start(bf16[256,128]{1,0:T(8,128)(2,1)S(1)} %get-tuple-element.39), channel_id=1, source_target_pairs={{0,1},{1,0},{2,3},{3,2},{4,5},{5,4},{6,7},{7,6},{8,9},{9,8},{10,11... | collective-permute-start | bytes 196616 | tf_op jit(solution)/shard_map/ppermute | solution.py:20
  34.4 0.0 collective-permute-done.5.refs_4_
  34.4 6.9 %collective-permute-start.10 = (bf16[256,128]{1,0:T(8,128)(2,1)S(1)}, bf16[256,128]{1,0:T(8,128)(2,1)S(1)}, u32[]{:S(2)}, u32[]{:S(2)}) collective-permute-start(bf16[256,128]{1,0:T(8,128)(2,1)S(1)} %get-tuple-element.40), channel_id=1, source_target_pairs={{0,2},{1,3},{2,0},{3,1},{4,6},{5,7},{6,4},{7,5},{8,10},{9,11},{10,... | collective-permute-start | bytes 196616 | tf_op jit(solution)/shard_map/ppermute | solution.py:20
  41.3 2.6 %collective-permute-done.6.refs_5_ = bf16[528,128]{1,0:T(8,128)(2,1)S(1)} collective-permute-done((bf16[528,128]{1,0:T(8,128)(2,1)S(1)}, bf16[528,128]{1,0:T(8,128)(2,1)S(1)}, u32[]{:S(2)}, u32[]{:S(2)}) %collective-permute-start.6) | collective-permute-done | bytes 135200 | tf_op jit(solution)/shard_map/ppermute | solution.py:20
  43.9 1.0 %collective-permute-start.11 = (bf16[256,128]{1,0:T(8,128)(2,1)S(1)}, bf16[256,128]{1,0:T(8,128)(2,1)S(1)}, u32[]{:S(2)}, u32[]{:S(2)}) collective-permute-start(bf16[256,128]{1,0:T(8,128)(2,1)S(1)} %get-tuple-element.41), channel_id=1, source_target_pairs={{0,3},{1,2},{2,1},{3,0},{4,7},{5,6},{6,5},{7,4},{8,11},{9,10},{10,... | collective-permute-start | bytes 196616 | tf_op jit(solution)/shard_map/ppermute | solution.py:20
  44.9 0.0 collective-permute-done.7.refs_6_
  44.9 4.8 %collective-permute-start.12 = (bf16[256,128]{1,0:T(8,128)(2,1)S(1)}, bf16[256,128]{1,0:T(8,128)(2,1)S(1)}, u32[]{:S(2)}, u32[]{:S(2)}) collective-permute-start(bf16[256,128]{1,0:T(8,128)(2,1)S(1)} %get-tuple-element.42), channel_id=1, source_target_pairs={{0,4},{1,5},{2,6},{3,7},{4,0},{5,1},{6,2},{7,3},{8,12},{9,13},{10,... | collective-permute-start | bytes 196616 | tf_op jit(solution)/shard_map/ppermute | solution.py:20
  49.7 0.0 collective-permute-done.8.refs_7_
  49.7 3.6 %collective-permute-start.13 = (bf16[256,128]{1,0:T(8,128)(2,1)S(1)}, bf16[256,128]{1,0:T(8,128)(2,1)S(1)}, u32[]{:S(2)}, u32[]{:S(2)}) collective-permute-start(bf16[256,128]{1,0:T(8,128)(2,1)S(1)} %get-tuple-element.43), channel_id=1, source_target_pairs={{0,5},{1,4},{2,7},{3,6},{4,1},{5,0},{6,3},{7,2},{8,13},{9,12},{10,... | collective-permute-start | bytes 196616 | tf_op jit(solution)/shard_map/ppermute | solution.py:20
  53.3 1.6 %join_b.1 = (bf16[2,1,6,128,128]{4,3,2,1,0:T(8,128)(2,1)}, f32[16,128]{1,0:T(8,128)S(1)}, bf16[2,6,32,128]{3,2,1,0:T(8,128)(2,1)S(1)}, bf16[2,6,32,128]{3,2,1,0:...) custom-call(s32[2]{0:T(128)S(1)} %pad_add_fusion.here, ...), custom_call_target="tpu_custom_call" | custom-call | flops 268435456 | bytes 1048576 | tf_op jit(solution)/shard_map/join_b/pallas_call | solution.py:176
  54.8 0.0 collective-permute-done.9.refs_1_
  54.8 0.0 collective-permute-start.16
  54.9 0.0 collective-permute-done.10.refs_2_
  54.9 0.6 collective-permute-start.17
  55.4 0.0 collective-permute-done.11.refs_3_
  55.4 1.3 %collective-permute-start.18 = (bf16[2,6,32,128]{3,2,1,0:T(8,128)(2,1)S(1)}, bf16[2,6,32,128]{3,2,1,0:T(8,128)(2,1)S(1)}, u32[]{:S(2)}, u32[]{:S(2)}) collective-permute-start(bf16[2,6,32,128]{3,2,1,0:T(8,128)(2,1)S(1)} %get-tuple-element.50), channel_id=1, source_target_pairs={{0,24},{8,16},{16,8},{24,0},{1,25},{9,17},{17,9},{25,1},{2,26},{10... | collective-permute-start | bytes 294920 | tf_op jit(solution)/shard_map/ppermute | solution.py:20
  56.7 0.0 collective-permute-done.12.refs_4_
  56.7 0.5 collective-permute-start.14
  57.2 0.0 collective-permute-done.13.refs_5_
  57.2 4.3 %collective-permute-start.15 = (bf16[256,128]{1,0:T(8,128)(2,1)S(1)}, bf16[256,128]{1,0:T(8,128)(2,1)S(1)}, u32[]{:S(2)}, u32[]{:S(2)}) collective-permute-start(bf16[256,128]{1,0:T(8,128)(2,1)S(1)} %get-tuple-element.45), channel_id=1, source_target_pairs={{0,7},{1,6},{2,5},{3,4},{4,3},{5,2},{6,1},{7,0},{8,15},{9,14},{10,... | collective-permute-start | bytes 196616 | tf_op jit(solution)/shard_map/ppermute | solution.py:20
  61.5 1.9 %collective-permute-done.14.refs_6_ = bf16[256,128]{1,0:T(8,128)(2,1)S(1)} collective-permute-done((bf16[256,128]{1,0:T(8,128)(2,1)S(1)}, bf16[256,128]{1,0:T(8,128)(2,1)S(1)}, u32[]{:S(2)}, u32[]{:S(2)}) %collective-permute-start.14) | collective-permute-done | bytes 65568 | tf_op jit(solution)/shard_map/ppermute | solution.py:20
  63.4 1.8 %collective-permute-done.15.refs_7_ = bf16[256,128]{1,0:T(8,128)(2,1)S(1)} collective-permute-done((bf16[256,128]{1,0:T(8,128)(2,1)S(1)}, bf16[256,128]{1,0:T(8,128)(2,1)S(1)}, u32[]{:S(2)}, u32[]{:S(2)}) %collective-permute-start.15) | collective-permute-done | bytes 65568 | tf_op jit(solution)/shard_map/ppermute | solution.py:20
  65.2 1.5 %join_g.1 = bf16[1,6,128,128]{3,2,1,0:T(8,128)(2,1)} custom-call(s32[2]{0:T(128)S(1)} %pad_add_fusion.here, s32[1,48]{1,0:T(1,128)S(1)} %copy-done.3, f32[16,128]{1,0:T(8,128)S(1)} %get-tuple-element.37.peak, bf16[256,128]{1,0:T(8,128)(2,1)S(1)} %get-tuple-element.38.refs_0_, bf16[256,128]{1,0:T(8,128)(2,1)S(1)} %collective-permute-done.9.refs_1_, ...), custom_call_target="tpu_custom_call" | custom-call | flops 268435456 | bytes 1048576 | tf_op jit(solution)/shard_map/join_g/pallas_call | solution.py:203
  66.7 0.0 collective-permute-done.16
  66.7 0.0 collective-permute-done.17
  66.7 0.0 collective-permute-done.18
  66.7 0.7 %convert_add_fusion = f32[2,6,32,128]{3,2,1,0:T(8,128)} fusion(bf16[2,6,32,128]{3,2,1,0:T(8,128)(2,1)S(1)} %collective-permute-done.18, bf16[2,6,32,128]{3,2,1,0:T(8,128)(2,1)S(1)} %collective-permute-done.17, bf16[2,6,32,128]{3,2,1,0:T(8,128)(2,1)S(1)} %collective-permute-done.16, bf16[2,6,32,128]{3,2,1,0:T(8,128)(2,1)S(1)} %get-tuple-element.47), kind=kLoop, calls=%fused_computation | loop fusion | flops 344064 | bytes 589824 | tf_op jit(solution)/shard_map/add | solution.py:236
  (5 shorter events, 0.0 us)
Async XLA Ops:
  0.6 16.3 %collective-permute-start.1 = (bf16[2,1,6,128,128]{4,3,2,1,0:T(8,128)(2,1)}, bf16[2,1,6,128,128]{4,3,2,1,0:T(8,128)(2,1)S(1)}, u32[]{:S(2)}, u32[]{:S(2)}) collective-permute-start(bf16[2,1,6,128,128]{4,3,2,1,0:T(8,128)(2,1)} %param.8), channel_id=1, source_target_pairs={{0,8},{8,16},{16,24},{24,0},{1,9},{9,17},{17,25},{25,1},{2,10},{10... | collective-permute-start | bytes 1179656 | tf_op jit(solution)/shard_map/ppermute | solution.py:221
  1.1 15.8 %collective-permute-start = (bf16[1,6,128,128]{3,2,1,0:T(8,128)(2,1)}, bf16[1,6,128,128]{3,2,1,0:T(8,128)(2,1)S(1)}, u32[]{:S(2)}, u32[]{:S(2)}) collective-permute-start(bf16[1,6,128,128]{3,2,1,0:T(8,128)(2,1)} %param.7), channel_id=1, source_target_pairs={{0,8},{8,16},{16,24},{24,0},{1,9},{9,17},{17,25},{25,1},{2,10},{10... | collective-permute-start | bytes 589832 | tf_op jit(solution)/shard_map/ppermute | solution.py:220
  4.6 2.0 %copy-start = (bf16[1,6,128,2304]{3,2,1,0:T(8,128)(2,1)S(1)}, bf16[1,6,128,2304]{3,2,1,0:T(8,128)(2,1)}, u32[]{:S(2)}) copy-start(bf16[1,6,128,2304]{3,2,1,0:T(8,128)(2,1)} %edge.1) | copy-start | bytes 10616836
  6.6 2.0 %copy-start.1 = (bf16[1,6,128,2304]{3,2,1,0:T(8,128)(2,1)S(1)}, bf16[1,6,128,2304]{3,2,1,0:T(8,128)(2,1)}, u32[]{:S(2)}) copy-start(bf16[1,6,128,2304]{3,2,1,0:T(8,128)(2,1)} %bedge.1) | copy-start | bytes 10616836
  8.6 2.0 %copy-start.2 = (bf16[1,6,2304,128]{3,2,1,0:T(8,128)(2,1)S(1)}, bf16[1,6,2304,128]{3,2,1,0:T(8,128)(2,1)}, u32[]{:S(2)}) copy-start(bf16[1,6,2304,128]{3,2,1,0:T(8,128)(2,1)} %proj.1) | copy-start | bytes 10616836
  10.7 6.3 %copy-start.3 = (s32[1,48]{1,0:T(1,128)S(1)}, s32[1,48]{1,0:T(1,128)}, u32[]{:S(2)}) copy-start(s32[1,48]{1,0:T(1,128)} %joining.5) | copy-start | bytes 580
  18.0 7.4 %collective-permute-start.2 = (bf16[528,128]{1,0:T(8,128)(2,1)S(1)}, bf16[528,128]{1,0:T(8,128)(2,1)S(1)}, u32[]{:S(2)}, u32[]{:S(2)}) collective-permute-start(bf16[528,128]{1,0:T(8,128)(2,1)S(1)} %get-tuple-element.30), channel_id=1, source_target_pairs={{0,1},{1,0},{2,3},{3,2},{4,5},{5,4},{6,7},{7,6},{8,9},{9,8},{10,11... | collective-permute-start | bytes 405512 | tf_op jit(solution)/shard_map/ppermute | solution.py:20
  19.6 11.1 %collective-permute-start.3 = (bf16[528,128]{1,0:T(8,128)(2,1)S(1)}, bf16[528,128]{1,0:T(8,128)(2,1)S(1)}, u32[]{:S(2)}, u32[]{:S(2)}) collective-permute-start(bf16[528,128]{1,0:T(8,128)(2,1)S(1)} %get-tuple-element.31), channel_id=1, source_target_pairs={{0,2},{1,3},{2,0},{3,1},{4,6},{5,7},{6,4},{7,5},{8,10},{9,11},{10,... | collective-permute-start | bytes 405512 | tf_op jit(solution)/shard_map/ppermute | solution.py:20
  21.2 10.9 %collective-permute-start.4 = (bf16[528,128]{1,0:T(8,128)(2,1)S(1)}, bf16[528,128]{1,0:T(8,128)(2,1)S(1)}, u32[]{:S(2)}, u32[]{:S(2)}) collective-permute-start(bf16[528,128]{1,0:T(8,128)(2,1)S(1)} %get-tuple-element.32), channel_id=1, source_target_pairs={{0,3},{1,2},{2,1},{3,0},{4,7},{5,6},{6,5},{7,4},{8,11},{9,10},{10,... | collective-permute-start | bytes 405512 | tf_op jit(solution)/shard_map/ppermute | solution.py:20
  21.6 12.8 %collective-permute-start.5 = (bf16[528,128]{1,0:T(8,128)(2,1)S(1)}, bf16[528,128]{1,0:T(8,128)(2,1)S(1)}, u32[]{:S(2)}, u32[]{:S(2)}) collective-permute-start(bf16[528,128]{1,0:T(8,128)(2,1)S(1)} %get-tuple-element.33), channel_id=1, source_target_pairs={{0,4},{1,5},{2,6},{3,7},{4,0},{5,1},{6,2},{7,3},{8,12},{9,13},{10,... | collective-permute-start | bytes 405512 | tf_op jit(solution)/shard_map/ppermute | solution.py:20
  24.2 19.7 %collective-permute-start.6 = (bf16[528,128]{1,0:T(8,128)(2,1)S(1)}, bf16[528,128]{1,0:T(8,128)(2,1)S(1)}, u32[]{:S(2)}, u32[]{:S(2)}) collective-permute-start(bf16[528,128]{1,0:T(8,128)(2,1)S(1)} %get-tuple-element.34), channel_id=1, source_target_pairs={{0,5},{1,4},{2,7},{3,6},{4,1},{5,0},{6,3},{7,2},{8,13},{9,12},{10,... | collective-permute-start | bytes 405512 | tf_op jit(solution)/shard_map/ppermute | solution.py:20
  25.4 19.5 %collective-permute-start.7 = (bf16[528,128]{1,0:T(8,128)(2,1)S(1)}, bf16[528,128]{1,0:T(8,128)(2,1)S(1)}, u32[]{:S(2)}, u32[]{:S(2)}) collective-permute-start(bf16[528,128]{1,0:T(8,128)(2,1)S(1)} %get-tuple-element.35), channel_id=1, source_target_pairs={{0,6},{1,7},{2,4},{3,5},{4,2},{5,3},{6,0},{7,1},{8,14},{9,15},{10,... | collective-permute-start | bytes 405512 | tf_op jit(solution)/shard_map/ppermute | solution.py:20
  30.6 19.1 %collective-permute-start.8 = (bf16[528,128]{1,0:T(8,128)(2,1)S(1)}, bf16[528,128]{1,0:T(8,128)(2,1)S(1)}, u32[]{:S(2)}, u32[]{:S(2)}) collective-permute-start(bf16[528,128]{1,0:T(8,128)(2,1)S(1)} %get-tuple-element.36), channel_id=1, source_target_pairs={{0,7},{1,6},{2,5},{3,4},{4,3},{5,2},{6,1},{7,0},{8,15},{9,14},{10,... | collective-permute-start | bytes 405512 | tf_op jit(solution)/shard_map/ppermute | solution.py:20
  32.1 22.8 %collective-permute-start.9 = (bf16[256,128]{1,0:T(8,128)(2,1)S(1)}, bf16[256,128]{1,0:T(8,128)(2,1)S(1)}, u32[]{:S(2)}, u32[]{:S(2)}) collective-permute-start(bf16[256,128]{1,0:T(8,128)(2,1)S(1)} %get-tuple-element.39), channel_id=1, source_target_pairs={{0,1},{1,0},{2,3},{3,2},{4,5},{5,4},{6,7},{7,6},{8,9},{9,8},{10,11... | collective-permute-start | bytes 196616 | tf_op jit(solution)/shard_map/ppermute | solution.py:20
  34.4 20.4 %collective-permute-start.10 = (bf16[256,128]{1,0:T(8,128)(2,1)S(1)}, bf16[256,128]{1,0:T(8,128)(2,1)S(1)}, u32[]{:S(2)}, u32[]{:S(2)}) collective-permute-start(bf16[256,128]{1,0:T(8,128)(2,1)S(1)} %get-tuple-element.40), channel_id=1, source_target_pairs={{0,2},{1,3},{2,0},{3,1},{4,6},{5,7},{6,4},{7,5},{8,10},{9,11},{10,... | collective-permute-start | bytes 196616 | tf_op jit(solution)/shard_map/ppermute | solution.py:20
  43.9 11.5 %collective-permute-start.11 = (bf16[256,128]{1,0:T(8,128)(2,1)S(1)}, bf16[256,128]{1,0:T(8,128)(2,1)S(1)}, u32[]{:S(2)}, u32[]{:S(2)}) collective-permute-start(bf16[256,128]{1,0:T(8,128)(2,1)S(1)} %get-tuple-element.41), channel_id=1, source_target_pairs={{0,3},{1,2},{2,1},{3,0},{4,7},{5,6},{6,5},{7,4},{8,11},{9,10},{10,... | collective-permute-start | bytes 196616 | tf_op jit(solution)/shard_map/ppermute | solution.py:20
  44.9 11.8 %collective-permute-start.12 = (bf16[256,128]{1,0:T(8,128)(2,1)S(1)}, bf16[256,128]{1,0:T(8,128)(2,1)S(1)}, u32[]{:S(2)}, u32[]{:S(2)}) collective-permute-start(bf16[256,128]{1,0:T(8,128)(2,1)S(1)} %get-tuple-element.42), channel_id=1, source_target_pairs={{0,4},{1,5},{2,6},{3,7},{4,0},{5,1},{6,2},{7,3},{8,12},{9,13},{10,... | collective-permute-start | bytes 196616 | tf_op jit(solution)/shard_map/ppermute | solution.py:20
  49.7 7.5 %collective-permute-start.13 = (bf16[256,128]{1,0:T(8,128)(2,1)S(1)}, bf16[256,128]{1,0:T(8,128)(2,1)S(1)}, u32[]{:S(2)}, u32[]{:S(2)}) collective-permute-start(bf16[256,128]{1,0:T(8,128)(2,1)S(1)} %get-tuple-element.43), channel_id=1, source_target_pairs={{0,5},{1,4},{2,7},{3,6},{4,1},{5,0},{6,3},{7,2},{8,13},{9,12},{10,... | collective-permute-start | bytes 196616 | tf_op jit(solution)/shard_map/ppermute | solution.py:20
  54.8 11.8 %collective-permute-start.16 = (bf16[2,6,32,128]{3,2,1,0:T(8,128)(2,1)S(1)}, bf16[2,6,32,128]{3,2,1,0:T(8,128)(2,1)S(1)}, u32[]{:S(2)}, u32[]{:S(2)}) collective-permute-start(bf16[2,6,32,128]{3,2,1,0:T(8,128)(2,1)S(1)} %get-tuple-element.48), channel_id=1, source_target_pairs={{0,8},{8,0},{16,24},{24,16},{1,9},{9,1},{17,25},{25,17},{2,10},{10... | collective-permute-start | bytes 294920 | tf_op jit(solution)/shard_map/ppermute | solution.py:20
  54.9 11.8 %collective-permute-start.17 = (bf16[2,6,32,128]{3,2,1,0:T(8,128)(2,1)S(1)}, bf16[2,6,32,128]{3,2,1,0:T(8,128)(2,1)S(1)}, u32[]{:S(2)}, u32[]{:S(2)}) collective-permute-start(bf16[2,6,32,128]{3,2,1,0:T(8,128)(2,1)S(1)} %get-tuple-element.49), channel_id=1, source_target_pairs={{0,16},{8,24},{16,0},{24,8},{1,17},{9,25},{17,1},{25,9},{2,18},{10... | collective-permute-start | bytes 294920 | tf_op jit(solution)/shard_map/ppermute | solution.py:20
  55.4 11.2 %collective-permute-start.18 = (bf16[2,6,32,128]{3,2,1,0:T(8,128)(2,1)S(1)}, bf16[2,6,32,128]{3,2,1,0:T(8,128)(2,1)S(1)}, u32[]{:S(2)}, u32[]{:S(2)}) collective-permute-start(bf16[2,6,32,128]{3,2,1,0:T(8,128)(2,1)S(1)} %get-tuple-element.50), channel_id=1, source_target_pairs={{0,24},{8,16},{16,8},{24,0},{1,25},{9,17},{17,9},{25,1},{2,26},{10... | collective-permute-start | bytes 294920 | tf_op jit(solution)/shard_map/ppermute | solution.py:20
  56.7 6.7 %collective-permute-start.14 = (bf16[256,128]{1,0:T(8,128)(2,1)S(1)}, bf16[256,128]{1,0:T(8,128)(2,1)S(1)}, u32[]{:S(2)}, u32[]{:S(2)}) collective-permute-start(bf16[256,128]{1,0:T(8,128)(2,1)S(1)} %get-tuple-element.44), channel_id=1, source_target_pairs={{0,6},{1,7},{2,4},{3,5},{4,2},{5,3},{6,0},{7,1},{8,14},{9,15},{10,... | collective-permute-start | bytes 196616 | tf_op jit(solution)/shard_map/ppermute | solution.py:20
  57.2 8.0 %collective-permute-start.15 = (bf16[256,128]{1,0:T(8,128)(2,1)S(1)}, bf16[256,128]{1,0:T(8,128)(2,1)S(1)}, u32[]{:S(2)}, u32[]{:S(2)}) collective-permute-start(bf16[256,128]{1,0:T(8,128)(2,1)S(1)} %get-tuple-element.45), channel_id=1, source_target_pairs={{0,7},{1,6},{2,5},{3,4},{4,3},{5,2},{6,1},{7,0},{8,15},{9,14},{10,... | collective-permute-start | bytes 196616 | tf_op jit(solution)/shard_map/ppermute | solution.py:20
